TPU v7x, 32 devices: a whole 2x2x4 slice. The times are simulated.
32 devices in a mesh: fsdp: 32 (over z, y, x, core).
Axes of the slice: x: 2, y: 2, z: 4, core: 2. Of those that a mesh axis runs over, the one named last changes fastest.
Arguments:
- token_ids: int32 [65536], P('fsdp'), may hold values from 0 to 14591
- masked: int32 [65536], P('fsdp'), may hold values 0 or 1
- swap_kind: int32 [65536], P('fsdp'), may hold values from 0 to 9
- swap_ids: int32 [65536], P('fsdp'), may hold values from 0 to 14591
- out_grad: bfloat16 [65536, 768], P('fsdp'), may hold values from -6 to 6
- embed_table: float32 [15104, 768], P('fsdp'), may hold values from -6 to 6
- table_first: float32 [15104, 768], P('fsdp'), may hold values from -16 to 16
- table_second: float32 [15104, 768], P('fsdp'), may hold values from 10 to 10000
- layer_mats: float32 [768, 9216], P(None, 'fsdp'), may hold values from -4 to 4
- mats_first: float32 [768, 9216], P(None, 'fsdp'), may hold values from -16 to 16
- mats_second: float32 [768, 9216], P(None, 'fsdp'), may hold values from 10 to 10000
- layer_vecs: float32 [9216], P('fsdp'), may hold values from -1.2 to 1.9
- vecs_first: float32 [9216], P('fsdp'), may hold values from -16 to 16
- vecs_second: float32 [9216], P('fsdp'), may hold values from 10 to 10000
Outputs:
- layer_out: bfloat16 [65536, 768], P('fsdp')
- input_grad: bfloat16 [65536, 768], P('fsdp')
- table_grad: float32 [15104, 768], P('fsdp')
- mats_grad: float32 [768, 9216], P(None, 'fsdp')
- vecs_grad: float32 [9216], P('fsdp')
- table_step: float32 [15104, 768], P('fsdp')
- table_first_next: float32 [15104, 768], P('fsdp')
- mats_step: float32 [768, 9216], P(None, 'fsdp')
- mats_first_next: float32 [768, 9216], P(None, 'fsdp')
- vecs_step: float32 [9216], P('fsdp')
- vecs_first_next: float32 [9216], P('fsdp')
Inputs may be any that keep to these rules, and one draw needn't show every extreme that they name: `swap_kind`: kinds 0 to 7 mean the mask token 103, kind 8 the id of swap_ids, kind 9 keeps the token's own id.
All inputs are finite; a program needn't handle non-finite values. No bound on the sum of `masked` on one device may be relied on, other than what follows from the above.
Results may differ from a plain program's by a relative error of at most 0.015.
The roundings to bfloat16 on the way count: a program that leaves them out, or rounds other values in their place, can miss the bound.
Values may be sent and summed in bfloat16 or wider, within the bound.
A program may use at most 320 MiB of HBM per device.

v0:
```python
import jax
import jax.numpy as jnp
from jax import lax
from jax.sharding import PartitionSpec as P

D = 768
HEADS = 12
HEAD_DIM = 64
FF = 3072
VOCAB = 14592
LENGTH = 512
STEP = 10
TABLE = 15104


norm_eps = 1e-12
mask_token = 103
beta_one = 0.9
beta_two = 0.999
adam_eps = 1e-06
decay_rate = 0.01


def matmul(left, right):
    return jnp.dot(left, right, preferred_element_type=jnp.float32)


def contract_rows(left, right):
    return lax.dot_general(
        left, right, (((0,), (0,)), ((), ())), preferred_element_type=jnp.float32
    )


def contract_cols(left, right):
    return lax.dot_general(
        left, right, (((1,), (1,)), ((), ())), preferred_element_type=jnp.float32
    )


def exact_gelu(values):
    return jax.nn.gelu(values, approximate=False)


def split_mats(weights):
    return (
        weights[:, : 3 * D],
        weights[:, 3 * D : 4 * D],
        weights[:, 4 * D : 4 * D + FF],
        weights[:, 4 * D + FF :],
    )


def split_vecs(biases):
    biases = biases.astype(jnp.float32)
    return (
        biases[0:D],
        biases[D : 2 * D],
        biases[2 * D : 3 * D],
        biases[3 * D : 4 * D],
        biases[4 * D : 5 * D],
        biases[5 * D : 5 * D + FF],
        biases[5 * D + FF : 6 * D + FF],
        biases[6 * D + FF : 7 * D + FF],
        biases[7 * D + FF : 8 * D + FF],
    )


def norm_parts(total, gain, shift):
    centre = jnp.mean(total, -1, keepdims=True)
    centered = total - centre
    variance = jnp.mean(centered * centered, -1, keepdims=True)
    scale = lax.rsqrt(variance + norm_eps)
    unit = centered * scale
    return (unit * gain + shift, unit, scale)


def norm_back(grad, gain, unit, scale):
    scaled = grad * gain
    return scale * (
        scaled
        - jnp.mean(scaled, -1, keepdims=True)
        - unit * jnp.mean(scaled * unit, -1, keepdims=True)
    )


def attention_forward(parts):
    query, keys, values = parts
    scores = jnp.einsum(
        "qhd,khd->hqk", query, keys, preferred_element_type=jnp.float32
    ) * HEAD_DIM ** (-0.5)
    highest = jnp.max(scores, -1, keepdims=True)
    expo = jnp.exp(scores - highest)
    total = jnp.sum(expo, -1, keepdims=True)
    probs = expo / total
    attended = jnp.einsum(
        "hqk,khd->qhd", probs.astype(jnp.bfloat16), values, preferred_element_type=jnp.float32
    )
    return (attended, highest + jnp.log(total))


def attention_backward(parts):
    query, keys, values, logsum, grad_att = parts
    scores = jnp.einsum(
        "qhd,khd->hqk", query, keys, preferred_element_type=jnp.float32
    ) * HEAD_DIM ** (-0.5)
    probs = jnp.exp(scores - logsum)
    grad_values = jnp.einsum(
        "hqk,qhd->khd", probs.astype(jnp.bfloat16), grad_att, preferred_element_type=jnp.float32
    )
    grad_probs = jnp.einsum("qhd,khd->hqk", grad_att, values, preferred_element_type=jnp.float32)
    grad_scores = probs * (grad_probs - jnp.sum(grad_probs * probs, -1, keepdims=True))
    grad_scores = grad_scores.astype(jnp.bfloat16)
    grad_query = jnp.einsum(
        "hqk,khd->qhd", grad_scores, keys, preferred_element_type=jnp.float32
    ) * HEAD_DIM ** (-0.5)
    grad_keys = jnp.einsum(
        "hqk,qhd->khd", grad_scores, query, preferred_element_type=jnp.float32
    ) * HEAD_DIM ** (-0.5)
    return jnp.stack([grad_query, grad_keys, grad_values], axis=1)


def adam_direction(param, first, second, grad, corr_one, corr_two, decay):
    first_next = beta_one * first + (1.0 - beta_one) * grad
    second_next = beta_two * second + (1.0 - beta_two) * grad * grad
    update = first_next / corr_one / (jnp.sqrt(second_next / corr_two) + adam_eps)
    return (update + decay * param, first_next)


def body(
    token_ids,
    masked,
    swap_kind,
    swap_ids,
    out_grad,
    embed_table,
    table_first,
    table_second,
    layer_mats,
    mats_first,
    mats_second,
    layer_vecs,
    vecs_first,
    vecs_second,
):
    rows = token_ids.shape[0]
    seqs = rows // LENGTH
    replaced = jnp.where(swap_kind < 8, mask_token, jnp.where(swap_kind == 8, swap_ids, token_ids))
    chosen = jnp.where(masked == 1, replaced, token_ids)
    places = VOCAB + jnp.arange(rows, dtype=jnp.int32) % LENGTH
    whole_table = lax.all_gather(embed_table.astype(jnp.bfloat16), "fsdp", axis=0, tiled=True)
    inputs = whole_table[chosen].astype(jnp.float32) + whole_table[places].astype(jnp.float32)
    mats_b, vecs_b = (
        lax.all_gather(layer_mats.astype(jnp.bfloat16), "fsdp", axis=1, tiled=True),
        lax.all_gather(layer_vecs.astype(jnp.bfloat16), "fsdp", axis=0, tiled=True),
    )
    w_qkv, w_out, w_up, w_down = split_mats(mats_b)
    (
        bias_query,
        bias_value,
        bias_out,
        gain_one,
        shift_one,
        bias_up,
        bias_down,
        gain_two,
        shift_two,
    ) = split_vecs(vecs_b)
    inputs_b = inputs.astype(jnp.bfloat16)
    projected = matmul(inputs_b, w_qkv) + jnp.concatenate(
        [bias_query, jnp.zeros((D,), jnp.float32), bias_value]
    )
    heads = projected.astype(jnp.bfloat16).reshape(seqs, LENGTH, 3, HEADS, HEAD_DIM)
    query = heads[:, :, 0]
    keys = heads[:, :, 1]
    values = heads[:, :, 2]
    attended, logsum = lax.map(attention_forward, (query, keys, values))
    attended_b = attended.reshape(rows, D).astype(jnp.bfloat16)
    branch = matmul(attended_b, w_out) + bias_out
    normed, unit_one, scale_one = norm_parts(inputs + branch, gain_one, shift_one)
    normed_b = normed.astype(jnp.bfloat16)
    upward = matmul(normed_b, w_up) + bias_up
    hidden_b = exact_gelu(upward).astype(jnp.bfloat16)
    downward = contract_cols(hidden_b, w_down) + bias_down
    outputs, unit_two, scale_two = norm_parts(normed + downward, gain_two, shift_two)
    mats_b, vecs_b = (
        lax.all_gather(layer_mats.astype(jnp.bfloat16), "fsdp", axis=1, tiled=True),
        lax.all_gather(layer_vecs.astype(jnp.bfloat16), "fsdp", axis=0, tiled=True),
    )
    w_qkv, w_out, w_up, w_down = split_mats(mats_b)
    (
        bias_query,
        bias_value,
        bias_out,
        gain_one,
        shift_one,
        bias_up,
        bias_down,
        gain_two,
        shift_two,
    ) = split_vecs(vecs_b)
    grad_out = out_grad.astype(jnp.float32) * masked.astype(jnp.float32)[:, None]
    grad_gain_two = jnp.sum(grad_out * unit_two, 0)
    grad_shift_two = jnp.sum(grad_out, 0)
    grad_mid = norm_back(grad_out, gain_two, unit_two, scale_two)
    grad_bias_down = jnp.sum(grad_mid, 0)
    grad_mid_b = grad_mid.astype(jnp.bfloat16)
    grad_w_down = contract_rows(grad_mid_b, hidden_b)
    grad_hidden = matmul(grad_mid_b, w_down)
    upward_again, slope_back = jax.vjp(exact_gelu, upward)
    (grad_upward,) = slope_back(grad_hidden)
    grad_bias_up = jnp.sum(grad_upward, 0)
    grad_upward_b = grad_upward.astype(jnp.bfloat16)
    grad_normed = grad_mid + contract_cols(grad_upward_b, w_up)
    grad_w_up = contract_rows(normed_b, grad_upward_b)
    grad_gain_one = jnp.sum(grad_normed * unit_one, 0)
    grad_shift_one = jnp.sum(grad_normed, 0)
    grad_first = norm_back(grad_normed, gain_one, unit_one, scale_one)
    grad_bias_out = jnp.sum(grad_first, 0)
    grad_first_b = grad_first.astype(jnp.bfloat16)
    grad_w_out = contract_rows(attended_b, grad_first_b)
    grad_att_b = (
        contract_cols(grad_first_b, w_out)
        .astype(jnp.bfloat16)
        .reshape(seqs, LENGTH, HEADS, HEAD_DIM)
    )
    grad_heads = lax.map(attention_backward, (query, keys, values, logsum, grad_att_b))
    grad_proj = grad_heads.reshape(rows, 3 * D)
    grad_bias_query = jnp.sum(grad_proj[:, :D], 0)
    grad_bias_value = jnp.sum(grad_proj[:, 2 * D :], 0)
    grad_proj_b = grad_proj.astype(jnp.bfloat16)
    grad_inputs = grad_first + contract_cols(grad_proj_b, w_qkv)
    grad_w_qkv = contract_rows(inputs_b, grad_proj_b)
    grad_mats = jnp.concatenate([grad_w_qkv, grad_w_out, grad_w_up, grad_w_down], axis=1)
    grad_vecs = jnp.concatenate(
        [
            grad_bias_query,
            grad_bias_value,
            grad_bias_out,
            grad_gain_one,
            grad_shift_one,
            grad_bias_up,
            grad_bias_down,
            grad_gain_two,
            grad_shift_two,
        ]
    )
    mats_grad, vecs_grad = (
        lax.psum_scatter(grad_mats, "fsdp", scatter_dimension=1, tiled=True),
        lax.psum_scatter(grad_vecs, "fsdp", scatter_dimension=0, tiled=True),
    )
    grad_table = (
        jnp.zeros((TABLE, D), jnp.float32).at[chosen].add(grad_inputs).at[places].add(grad_inputs)
    )
    table_grad = lax.psum_scatter(grad_table, "fsdp", scatter_dimension=0, tiled=True)
    counter = jnp.float32(STEP)
    corr_one = 1.0 - jnp.power(jnp.float32(beta_one), counter)
    corr_two = 1.0 - jnp.power(jnp.float32(beta_two), counter)
    table_step, table_first_next = adam_direction(
        embed_table, table_first, table_second, table_grad, corr_one, corr_two, decay_rate
    )
    mats_step, mats_first_next = adam_direction(
        layer_mats, mats_first, mats_second, mats_grad, corr_one, corr_two, decay_rate
    )
    vecs_step, vecs_first_next = adam_direction(
        layer_vecs, vecs_first, vecs_second, vecs_grad, corr_one, corr_two, 0.0
    )
    return (
        outputs.astype(jnp.bfloat16),
        grad_inputs.astype(jnp.bfloat16),
        table_grad,
        mats_grad,
        vecs_grad,
        table_step,
        table_first_next,
        mats_step,
        mats_first_next,
        vecs_step,
        vecs_first_next,
    )


def solution(mesh):
    return jax.shard_map(
        body,
        mesh=mesh,
        in_specs=(
            P("fsdp"),
            P("fsdp"),
            P("fsdp"),
            P("fsdp"),
            P("fsdp", None),
            P("fsdp", None),
            P("fsdp", None),
            P("fsdp", None),
            P(None, "fsdp"),
            P(None, "fsdp"),
            P(None, "fsdp"),
            P("fsdp"),
            P("fsdp"),
            P("fsdp"),
        ),
        out_specs=(
            P("fsdp", None),
            P("fsdp", None),
            P("fsdp", None),
            P(None, "fsdp"),
            P("fsdp"),
            P("fsdp", None),
            P("fsdp", None),
            P(None, "fsdp"),
            P(None, "fsdp"),
            P("fsdp"),
            P("fsdp"),
        ),
        check_vma=False,
    )
```

profile of v0, /device:TPU:0, one launch (start us, length us, event | category | flops | bytes accessed | tf_op | source)
XLA Modules:
  0.0 1875.5 jit_solution(12075779069803507719)
XLA Ops:
  12.8 43.4 %all-reduce = bf16[9216]{0:T(1024)(128)(2,1)S(1)} all-reduce(bf16[9216]{0:T(1024)(128)(2,1)S(1)} %dynamic-update-slice), channel_id=1, replica_groups=mesh['fsdp'=32] {'fsdp'}, use_global_device_ids=true, to_apply=%add | all-reduce | flops 9216 | bytes 36864
  61.5 99.6 %all-gather.3.cloned.1.call-done = bf16[15104,768]{1,0:T(8,128)(2,1)} async-done(((bf16[472,768]{1,0:T(8,128)(2,1)}), bf16[15104,768]{1,0:T(8,128)(2,1)}) %all-gather.3.cloned.1.call-update) | async-done | bytes 23199760 | tf_op jit(solution)/shard_map/all_gather | solution.py:150
  161.1 19.0 %gather_fusion = bf16[2048,768]{1,0:T(8,128)(2,1)S(1)} fusion(bf16[15104,768]{1,0:T(8,128)(2,1)} %all-gather.3.cloned.1.call-done, s32[2048]{0:T(1024)S(1)} %get-tuple-element.196), kind=kCustom, calls=%fused_computation | custom fusion | bytes 6299648 | tf_op jit(solution)/shard_map/gather | solution.py:151
  183.1 19.0 %gather_fusion.1 = bf16[2048,768]{1,0:T(8,128)(2,1)S(1)} fusion(bf16[15104,768]{1,0:T(8,128)(2,1)} %all-gather.3.cloned.1.call-done, s32[2048]{0:T(1024)S(1)} %broadcast_clamp_fusion), kind=kCustom, calls=%fused_computation.1 | custom fusion | bytes 6299648 | tf_op jit(solution)/shard_map/gather | solution.py:151
  205.1 60.9 %all-gather.5.cloned.1.call-done = bf16[768,9216]{0,1:T(8,128)(2,1)} async-done(((bf16[768,288]{0,1:T(8,128)(2,1)}), bf16[768,9216]{0,1:T(8,128)(2,1)}) %all-gather.5.cloned.1.call-update) | async-done | bytes 14155792 | tf_op jit(solution)/shard_map/all_gather | solution.py:153
  320.3 42.2 %while.22 = (s32[]{:T(128)}, bf16[4,512,12,64]{1,3,2,0:T(8,128)(2,1)}, f32[4,12,512,1]{2,1,3,0:T(8,128)}, bf16[4,512,12,64]{1,3,2,0:T(8,128)(2,1)}, bf16[4,512,1...) while((s32[]{:T(128)}, bf16[4,512,12,64]{1,3,2,0:T(8,128)(2,1)}, ...), condition=%wide.region_3.4_spmd, body=%wide.region_0.3_spmd.sunk | while | flops 833611776 | bytes 41888332 | solution.py:176
  376.8 65.8 %multiply_convert_fusion.1 = (bf16[2048,3072]{1,0:T(8,128)(2,1)}, f32[2048,3072]{1,0:T(8,128)}, f32[2048,3072]{1,0:T(8,128)}) fusion(f32[3072]{0:T(1024)S(1)} %copy-done.40, bf16[768,9216]{0,1:T(8,128)(2,1)} %all-gather.5.cloned.1.call-done, bf16[2048,768]{0,1:T(8,128)(2,1)S(1)} %fusion.112.clone.5), kind=kOutput, calls=%fused_computation.59 | convolution fusion | flops 10078912512 | bytes 70791168 | tf_op jit(solution)/shard_map/dot_general | solution.py:25
  442.6 18.0 fusion.118
  483.9 32.6 %fusion.120 = (f32[3072]{0:T(1024)}, bf16[2048,3072]{1,0:T(8,128)(2,1)}) fusion(f32[2048,3072]{1,0:T(8,128)} %get-tuple-element.195, bf16[768,9216]{0,1:T(8,128)(2,1)} %all-gather.5.cloned.1.call-done, f32[2048]{0:T(1024)S(1)} %get-tuple-element.227, f32[2048,768]{0,1:T(8,128)} %get-tuple-element.221, f32[2048]{0:T(1024)S(1)} %broadcast_multiply_fusion.4, ...), kind=kOutput, calls=%fused_computation.186 | convolution fusion | flops 9780065280 | bytes 77138944 | tf_op jit(solution)/shard_map/dot_general | solution.py:25
  533.7 23.1 %multiply_reduce_fusion.3 = (f32[768]{0:T(1024)}, f32[2048]{0:T(1024)S(1)}, f32[2048]{0:T(1024)S(1)}, f32[768]{0:T(1024)}, f32[2048,768]{0,1:T(8,128)}) fusion(f32[2048,768]{0,1:T(8,128)} %copy-done.3, f32[2048]{0:T(1024)S(1)} %copy-done.24, f32[2048]{0:T(1024)S(1)} %copy-done.18, f32[768]{0:T(1024)S(1)} %copy-done.30, ...), kind=kOutput, calls=%fused_computation.79 | convolution fusion | flops 9693554688 | bytes 39407616 | tf_op jit(solution)/shard_map/dot_general | solution.py:35
  585.0 524.1 %while.23 = (s32[]{:T(128)}, f32[4,512,3,12,64]{1,0,4,3,2:T(4,128)}, bf16[4,512,12,64]{1,3,2,0:T(8,128)(2,1)}, bf16[4,512,12,64]{1,3,2,0:T(8,128)(2,1)S(1)}, f32...) while((s32[]{:T(128)}, ...), condition=%wide.region_14.15_spmd, body=%wide.region_12.14_spmd.sunk | while | flops 2054154240 | bytes 133082208 | solution.py:226
  625.4 90.9 %dynamic_update_slice.19 = f32[4,512,3,12,64]{1,0,4,3,2:T(4,128)} dynamic-update-slice(f32[4,512,3,12,64]{1,0,4,3,2:T(4,128)} %get-tuple-element.350, f32[1,512,3,12,64]{1,0,4,3,2:T(1,128)} %copy.144, s32[]{:T(128)} %get-tuple-element.349, s32[]{:T(128)} %constant.75.clone.1..sunk, s32[]{:T(128)} %constant.75.clone.1..sunk, s32[]{:T(128)} %constant.75.clone.1..sunk, s32[]{:T(128)} %constant.75.clone.1..sunk) | dynamic-update-slice | bytes 9437188 | tf_op jit(solution)/shard_map/while/body/jit(dynamic_update_index_in_dim)/dynamic_update_slice | solution.py:226
  756.3 90.9 %dynamic_update_slice.19 = f32[4,512,3,12,64]{1,0,4,3,2:T(4,128)} dynamic-update-slice(f32[4,512,3,12,64]{1,0,4,3,2:T(4,128)} %get-tuple-element.350, f32[1,512,3,12,64]{1,0,4,3,2:T(1,128)} %copy.144, s32[]{:T(128)} %get-tuple-element.349, s32[]{:T(128)} %constant.75.clone.1..sunk, s32[]{:T(128)} %constant.75.clone.1..sunk, s32[]{:T(128)} %constant.75.clone.1..sunk, s32[]{:T(128)} %constant.75.clone.1..sunk) | dynamic-update-slice | bytes 9437188 | tf_op jit(solution)/shard_map/while/body/jit(dynamic_update_index_in_dim)/dynamic_update_slice | solution.py:226
  887.2 90.9 %dynamic_update_slice.19 = f32[4,512,3,12,64]{1,0,4,3,2:T(4,128)} dynamic-update-slice(f32[4,512,3,12,64]{1,0,4,3,2:T(4,128)} %get-tuple-element.350, f32[1,512,3,12,64]{1,0,4,3,2:T(1,128)} %copy.144, s32[]{:T(128)} %get-tuple-element.349, s32[]{:T(128)} %constant.75.clone.1..sunk, s32[]{:T(128)} %constant.75.clone.1..sunk, s32[]{:T(128)} %constant.75.clone.1..sunk, s32[]{:T(128)} %constant.75.clone.1..sunk) | dynamic-update-slice | bytes 9437188 | tf_op jit(solution)/shard_map/while/body/jit(dynamic_update_index_in_dim)/dynamic_update_slice | solution.py:226
  1018.1 90.9 %dynamic_update_slice.19 = f32[4,512,3,12,64]{1,0,4,3,2:T(4,128)} dynamic-update-slice(f32[4,512,3,12,64]{1,0,4,3,2:T(4,128)} %get-tuple-element.350, f32[1,512,3,12,64]{1,0,4,3,2:T(1,128)} %copy.144, s32[]{:T(128)} %get-tuple-element.349, s32[]{:T(128)} %constant.75.clone.1..sunk, s32[]{:T(128)} %constant.75.clone.1..sunk, s32[]{:T(128)} %constant.75.clone.1..sunk, s32[]{:T(128)} %constant.75.clone.1..sunk) | dynamic-update-slice | bytes 9437188 | tf_op jit(solution)/shard_map/while/body/jit(dynamic_update_index_in_dim)/dynamic_update_slice | solution.py:226
  1109.1 19.0 %copy.142 = f32[288,8,4,512]{3,1,2,0:T(8,128)} copy(f32[288,8,4,512]{3,2,1,0:T(4,128)} %bitcast.131) | data formatting | bytes 37748736
  1143.3 19.3 %pad_maximum_fusion = f32[768,9216]{1,0:T(8,128)} fusion(f32[768,3072]{1,0:T(8,128)} %fusion.84, f32[768,3072]{1,0:T(8,128)} %fusion.50, f32[768,768]{1,0:T(8,128)} %fusion.81, f32[768,2304]{1,0:T(8,128)} %fusion.59), kind=kLoop, calls=%fused_computation.56 | loop fusion | flops 21233664 | bytes 56623104 | tf_op jit(solution)/shard_map/concatenate | solution.py:233
  1162.6 27.7 %copy.120 = f32[768,9216]{0,1:T(8,128)} copy(f32[768,9216]{1,0:T(8,128)} %pad_maximum_fusion) | data formatting | bytes 56623104
  1190.4 18.2 fusion.119
  1215.6 35.9 %scatter_custom_fusion = f32[15104,768]{1,0:T(8,128)} fusion(s32[2048]{0:T(1024)} %get-tuple-element.197, f32[2048,768]{1,0:T(8,128)} %copy.101, f32[]{:T(128)} %constant.81.clone.1), kind=kCustom, calls=%fused_computation.73 | custom fusion | flops 1572864 | bytes 46400000 | tf_op jit(solution)/shard_map/scatter-add | solution.py:252
  1251.5 46.8 %scatter_fusion = f32[15104,768]{1,0:T(8,128)} fusion(f32[15104,768]{1,0:T(8,128)} %scatter_custom_fusion, s32[2048]{0:T(1024)S(1)} %bitcast.138, f32[2048,768]{1,0:T(8,128)} %copy.101), kind=kCustom, calls=%fused_computation.3 | custom fusion | flops 1572864 | bytes 18882560 | tf_op jit(solution)/shard_map/scatter-add | solution.py:252
  1328.8 38.6 %all-reduce.1 = f32[9216]{0:T(1024)S(1)} all-reduce(f32[9216]{0:T(1024)S(1)} %constant_dynamic-update-slice_fusion), channel_id=4, replica_groups=mesh['fsdp'=32] {'fsdp'}, use_global_device_ids=true, to_apply=%region_28.29.clone | all-reduce | flops 9216 | bytes 73728
  1368.2 84.8 %reduce-scatter.7.cloned.1.call-done = f32[288,768]{1,0:T(8,128)} async-done(((f32[9216,768]{1,0:T(8,128)}), f32[288,768]{1,0:T(8,128)}) %reduce-scatter.7.cloned.1.call-update) | async-done | bytes 884752
  1464.9 398.9 %reduce-scatter.5.cloned.1.call-done = f32[472,768]{1,0:T(8,128)} async-done(((f32[15104,768]{1,0:T(8,128)}), f32[472,768]{1,0:T(8,128)}) %reduce-scatter.5.cloned.1.call-update) | async-done | bytes 1450000 | tf_op jit(solution)/shard_map/reduce_scatter | solution.py:254
  (236 shorter events, 425.1 us)
Async XLA Ops:
  7.2 49.6 %copy-start.9 = (bf16[2048,768]{1,0:T(8,128)(2,1)S(1)}, bf16[2048,768]{1,0:T(8,128)(2,1)}, u32[]{:S(2)}) copy-start(bf16[2048,768]{1,0:T(8,128)(2,1)} %param.22) | copy-start | bytes 9437188
  7.2 53.7 %copy-start.41 = (s32[2048]{0:T(1024)S(1)}, s32[2048]{0:T(1024)}, u32[]{:S(2)}) copy-start(s32[2048]{0:T(1024)} %param.18) | copy-start | bytes 24580
  7.2 53.7 %copy-start.44 = (s32[2048]{0:T(1024)S(1)}, s32[2048]{0:T(1024)}, u32[]{:S(2)}) copy-start(s32[2048]{0:T(1024)} %param.19) | copy-start | bytes 24580
  7.2 53.7 %copy-start.43 = (s32[2048]{0:T(1024)S(1)}, s32[2048]{0:T(1024)}, u32[]{:S(2)}) copy-start(s32[2048]{0:T(1024)} %param.20) | copy-start | bytes 24580
  7.2 53.7 %copy-start.42 = (s32[2048]{0:T(1024)S(1)}, s32[2048]{0:T(1024)}, u32[]{:S(2)}) copy-start(s32[2048]{0:T(1024)} %param.21) | copy-start | bytes 24580
  7.2 153.9 %all-gather.3.cloned.1.call-start = ((), (), s32[]{:S(2)}) async-start(), calls=%async_computation.2 | async-start | bytes 23924736 | tf_op jit(solution)/shard_map/all_gather | solution.py:150
  9.7 256.3 %all-gather.5.cloned.1.call-start = ((), (), s32[]{:S(2)}) async-start(), calls=%async_computation.3 | async-start | bytes 14598144 | tf_op jit(solution)/shard_map/all_gather | solution.py:153
  11.8 1441.2 %reduce-scatter.7.cloned.1.call-start = ((), (), s32[]{:S(2)}) async-start(), calls=%async_computation.5 | async-start | bytes 29196288
  374.9 67.7 %copy-start.23 = (f32[2048]{0:T(1024)}, f32[2048]{0:T(1024)S(1)}, u32[]{:S(2)}) copy-start(f32[2048]{0:T(1024)S(1)} %add_rsqrt_fusion.1) | copy-start | bytes 24580
  376.8 65.8 %copy-start.30 = (f32[768]{0:T(1024)S(1)}, f32[768]{0:T(1024)}, u32[]{:S(2)}) copy-start(f32[768]{0:T(1024)} %get-tuple-element.211) | copy-start | bytes 9220
  376.8 65.8 %copy-start.37 = (f32[768]{0:T(1024)S(1)}, f32[768]{0:T(1024)}, u32[]{:S(2)}) copy-start(f32[768]{0:T(1024)} %get-tuple-element.212) | copy-start | bytes 9220
  376.8 65.8 %copy-start.46 = (f32[768]{0:T(1024)S(1)}, f32[768]{0:T(1024)}, u32[]{:S(2)}) copy-start(f32[768]{0:T(1024)} %get-tuple-element.210) | copy-start | bytes 9220
  460.6 73.0 %copy-start.15 = (f32[2048]{0:T(1024)}, f32[2048]{0:T(1024)S(1)}, u32[]{:S(2)}) copy-start(f32[2048]{0:T(1024)S(1)} %broadcast_multiply_fusion.4) | copy-start | bytes 24580
  464.2 69.4 %copy-start.21 = (f32[2048]{0:T(1024)}, f32[2048]{0:T(1024)S(1)}, u32[]{:S(2)}) copy-start(f32[2048]{0:T(1024)S(1)} %add_rsqrt_fusion) | copy-start | bytes 24580
  467.8 65.9 %copy-start.31 = (f32[2048]{0:T(1024)}, f32[2048]{0:T(1024)S(1)}, u32[]{:S(2)}) copy-start(f32[2048]{0:T(1024)S(1)} %get-tuple-element.227) | copy-start | bytes 24580
  467.8 65.9 %copy-start.33 = (f32[2048]{0:T(1024)}, f32[2048]{0:T(1024)S(1)}, u32[]{:S(2)}) copy-start(f32[2048]{0:T(1024)S(1)} %get-tuple-element.228) | copy-start | bytes 24580
  483.9 32.6 %copy-start.24 = (f32[2048]{0:T(1024)S(1)}, f32[2048]{0:T(1024)}, u32[]{:S(2)}) copy-start(f32[2048]{0:T(1024)} %copy-done.23) | copy-start | bytes 24580
  1190.3 673.5 %reduce-scatter.5.cloned.1.call-start = ((), (), s32[]{:S(2)}) async-start(), calls=%async_computation.4 | async-start | bytes 47849472 | tf_op jit(solution)/shard_map/reduce_scatter | solution.py:254
  1215.6 35.9 %copy-start.26 = (s32[2048,1]{0,1:T(1,128)S(1)}, s32[2048,1]{0,1:T(1,128)}, u32[]{:S(2)}) copy-start(s32[2048,1]{0,1:T(1,128)} %copy-done.25) | copy-start | bytes 24580
  1323.0 44.4 %copy-start.45 = (f32[288]{0:T(512)S(1)}, f32[288]{0:T(512)}, u32[]{:S(2)}) copy-start(f32[288]{0:T(512)} %param.29) | copy-start | bytes 3460
  1323.0 44.4 %copy-start.50 = (f32[288]{0:T(512)S(1)}, f32[288]{0:T(512)}, u32[]{:S(2)}) copy-start(f32[288]{0:T(512)} %param.31) | copy-start | bytes 3460
  1323.1 44.4 %copy-start.51 = (f32[288]{0:T(512)S(1)}, f32[288]{0:T(512)}, u32[]{:S(2)}) copy-start(f32[288]{0:T(512)} %param.30) | copy-start | bytes 3460
  1323.1 132.6 %copy-start.8 = (f32[768,288]{1,0:T(8,128)S(1)}, f32[768,288]{1,0:T(8,128)}, u32[]{:S(2)}) copy-start(f32[768,288]{1,0:T(8,128)} %copy.106) | copy-start | bytes 2654212
  1453.0 410.8 %copy-start.7 = (f32[472,768]{1,0:T(8,128)S(1)}, f32[472,768]{1,0:T(8,128)}, u32[]{:S(2)}) copy-start(f32[472,768]{1,0:T(8,128)} %param.23) | copy-start | bytes 4349956
  (32 other events, 272.6 us)
Sparse Core Ops, SparseCore 0:
  11.5 149.5 all-gather.2
  164.6 101.3 all-gather.4
  1190.4 262.5 reduce-scatter.6
  1459.8 403.8 reduce-scatter.4
where the time goes:
time: 1900 us; the launch traced here: 1880 us
  waiting for transfers between devices  644 us (34%)
  local copies, waits for them, and re-layouts  595 us (31%)
  matrix products  343 us (18%)
  other arithmetic  195 us (10%)
  blocking collectives  82.1 us (4%)
    dynamic_update_slice x8, local copies, waits for them, and re-layouts, body(): lax.map(attention_backward, (query, keys, values, logsum, grad_att_b))  402 us
    reduce_scatter x1, waiting for transfers between devices, body(): lax.psum_scatter(grad_table, 'fsdp', scatter_dimension=0, tiled=True)  399 us
    dot_general x4, matrix products, matmul(): return jnp.dot(left, right, preferred_element_type=jnp.float32)  117 us
    all_gather x1, waiting for transfers between devices, body(): lax.all_gather(embed_table.astype(jnp.bfloat16), 'fsdp', axis=0, tiled=True)  99.6 us
    unnamed x5, waiting for transfers between devices  84.9 us
    scatter-add x2, other arithmetic, body(): jnp.zeros((TABLE, D), jnp.float32).at[chosen].add(grad_inputs).at[places]  82.7 us
    unnamed x2, blocking collectives  82.1 us
    unnamed x126, local copies, waits for them, and re-layouts  78.3 us
  transfers between devices with their start and end apart: 4, of which 4 were waited for; matrix products, arithmetic and copies ran while one was open for 11% of the time, Pallas kernels for 0%

commit v1 on v0

v1 whole, which is shorter than its diff:
```python
import functools

import jax
import jax.numpy as jnp
from jax import lax
from jax.experimental import pallas as pl
from jax.experimental.pallas import tpu as pltpu
from jax.sharding import PartitionSpec as P

D = 768
HEADS = 12
HEAD_DIM = 64
FF = 3072
VOCAB = 14592
LENGTH = 512
STEP = 10
QKV = 3 * D

norm_eps = 1e-12
mask_token = 103
beta_one = 0.9
beta_two = 0.999
adam_eps = 1e-06
decay_rate = 0.01

BF = jnp.bfloat16
F32 = jnp.float32
LOG2E = 1.4426950408889634
SCORE = HEAD_DIM ** (-0.5)
MB = 1024 * 1024

ROW_TILE = 256
FF_TILE = 768


def dot_nn(left, right):
    return lax.dot_general(
        left, right, (((1,), (0,)), ((), ())), preferred_element_type=F32
    )


def dot_nt(left, right):
    return lax.dot_general(
        left, right, (((1,), (1,)), ((), ())), preferred_element_type=F32
    )


def dot_tn(left, right):
    return lax.dot_general(
        left, right, (((0,), (0,)), ((), ())), preferred_element_type=F32
    )


def attention_forward_kernel(q_ref, k_ref, v_ref, att_ref, lse_ref):
    query = q_ref[...]
    keys = k_ref[...]
    values_t = v_ref[...].T
    lane = lax.broadcasted_iota(jnp.int32, query.shape, 1)
    outs = []
    for half in range(2):
        mine = (lane < HEAD_DIM) if half == 0 else (lane >= HEAD_DIM)
        picked = jnp.where(mine, query, jnp.zeros_like(query))
        scores = dot_nt(keys, picked)
        highest = jnp.max(scores, 0, keepdims=True)
        expo = jnp.exp2((scores - highest) * (SCORE * LOG2E))
        total = jnp.sum(expo, 0, keepdims=True)
        part = values_t[half * HEAD_DIM : (half + 1) * HEAD_DIM, :]
        outs.append(dot_nn(part, expo.astype(BF)) / total)
        lse_ref[0, half : half + 1, :] = highest * (SCORE * LOG2E) + jnp.log2(total)
    att_ref[...] = jnp.concatenate(outs, 0).T.astype(BF)


def attention_forward(projected):
    rows = projected.shape[0]
    seqs = rows // LENGTH
    pairs = HEADS // 2
    block = (LENGTH, 2 * HEAD_DIM)
    return pl.pallas_call(
        attention_forward_kernel,
        grid=(seqs, pairs),
        in_specs=[
            pl.BlockSpec(block, lambda s, h: (s, h)),
            pl.BlockSpec(block, lambda s, h: (s, pairs + h)),
            pl.BlockSpec(block, lambda s, h: (s, 2 * pairs + h)),
        ],
        out_specs=[
            pl.BlockSpec(block, lambda s, h: (s, h)),
            pl.BlockSpec((1, 2, LENGTH), lambda s, h: (s * pairs + h, 0, 0)),
        ],
        out_shape=[
            jax.ShapeDtypeStruct((rows, D), BF),
            jax.ShapeDtypeStruct((seqs * pairs, 2, LENGTH), F32),
        ],
        compiler_params=pltpu.CompilerParams(vmem_limit_bytes=48 * MB),
        name="attention_forward",
    )(projected, projected, projected)


def attention_backward_kernel(
    q_ref, k_ref, v_ref, att_ref, g_ref, lse_ref, out_ref, bias_ref
):
    query = q_ref[...]
    keys = k_ref[...]
    values = v_ref[...]
    grad = g_ref[...]
    lane = lax.broadcasted_iota(jnp.int32, query.shape, 1)
    first = lane < HEAD_DIM
    product = (att_ref[...].astype(F32) * grad.astype(F32)).T
    zero = jnp.zeros_like(query)
    g_q, g_k, g_v = [], [], []
    for half in range(2):
        mine = first if half == 0 else jnp.logical_not(first)
        scores = dot_nt(keys, jnp.where(mine, query, zero))
        probs = jnp.exp2(scores * (SCORE * LOG2E) - lse_ref[0, half : half + 1, :])
        delta = jnp.sum(
            product[half * HEAD_DIM : (half + 1) * HEAD_DIM, :], 0, keepdims=True
        )
        g_probs = dot_nt(values, jnp.where(mine, grad, zero))
        g_v.append(dot_nn(probs.astype(BF), grad))
        g_scores = (probs * (g_probs - delta)).astype(BF)
        g_k.append(dot_nn(g_scores, query))
        g_q.append(dot_tn(g_scores, keys))
    grad_q = jnp.where(first, g_q[0], g_q[1]) * SCORE
    grad_k = jnp.where(first, g_k[0], g_k[1]) * SCORE
    grad_v = jnp.where(first, g_v[0], g_v[1])
    out_ref[0] = grad_q.astype(BF)
    out_ref[1] = grad_k.astype(BF)
    out_ref[2] = grad_v.astype(BF)

    @pl.when(pl.program_id(1) == 0)
    def _():
        bias_ref[...] = jnp.zeros_like(bias_ref)

    bias_ref[0:1, :] += jnp.sum(grad_q, 0, keepdims=True)
    bias_ref[1:2, :] += jnp.sum(grad_v, 0, keepdims=True)


def attention_backward(projected, attended, grad_att, lse):
    rows = projected.shape[0]
    seqs = rows // LENGTH
    pairs = HEADS // 2
    block = (LENGTH, 2 * HEAD_DIM)
    return pl.pallas_call(
        attention_backward_kernel,
        grid=(pairs, seqs),
        in_specs=[
            pl.BlockSpec(block, lambda h, s: (s, h)),
            pl.BlockSpec(block, lambda h, s: (s, pairs + h)),
            pl.BlockSpec(block, lambda h, s: (s, 2 * pairs + h)),
            pl.BlockSpec(block, lambda h, s: (s, h)),
            pl.BlockSpec(block, lambda h, s: (s, h)),
            pl.BlockSpec((1, 2, LENGTH), lambda h, s: (s * pairs + h, 0, 0)),
        ],
        out_specs=[
            pl.BlockSpec((3,) + block, lambda h, s: (0, s, h)),
            pl.BlockSpec((8, 2 * HEAD_DIM), lambda h, s: (0, h)),
        ],
        out_shape=[
            jax.ShapeDtypeStruct((3, rows, D), BF),
            jax.ShapeDtypeStruct((8, D), F32),
        ],
        compiler_params=pltpu.CompilerParams(vmem_limit_bytes=48 * MB),
        name="attention_backward",
    )(projected, projected, projected, attended, grad_att, lse)


def gelu_parts(values):
    size = jnp.abs(values)
    frac = 1.0 / (1.0 + (0.3275911 * 0.7071067811865476) * size)
    expo = jnp.exp2(values * values * (-0.5 * LOG2E))
    poly = 1.061405429 * 0.5
    for coef in (-1.453152027, 1.421413741, -0.284496736, 0.254829592):
        poly = poly * frac + 0.5 * coef
    tail = poly * frac * expo
    cdf = jnp.where(values >= 0, 1.0 - tail, tail)
    return values * cdf, cdf + values * expo * 0.3989422804014327


def norm_parts(total):
    centre = jnp.mean(total, -1, keepdims=True)
    centered = total - centre
    variance = jnp.mean(centered * centered, -1, keepdims=True)
    scale = lax.rsqrt(variance + norm_eps)
    return centered * scale, scale


def norm_back(scaled, unit, scale):
    return scale * (
        scaled
        - jnp.mean(scaled, -1, keepdims=True)
        - unit * jnp.mean(scaled * unit, -1, keepdims=True)
    )


def middle_kernel(
    att_ref,
    x_ref,
    go_ref,
    mask_ref,
    wout_ref,
    wup_ref,
    wdown_ref,
    vec_ref,
    bup_ref,
    out_ref,
    normed_ref,
    hidden_ref,
    gmid_ref,
    gup_ref,
    gfirst_ref,
    gfirstb_ref,
    gatt_ref,
    sums_ref,
    slope_ref,
):
    @pl.when(pl.program_id(0) == 0)
    def _():
        sums_ref[...] = jnp.zeros_like(sums_ref)

    bias_out = vec_ref[0:1, :]
    gain_one = vec_ref[1:2, :]
    shift_one = vec_ref[2:3, :]
    bias_down = vec_ref[3:4, :]
    gain_two = vec_ref[4:5, :]
    shift_two = vec_ref[5:6, :]

    def note(row, values):
        sums_ref[row : row + 1, 0:D] += jnp.sum(values, 0, keepdims=True)

    branch = dot_nt(att_ref[...], wout_ref[...]) + bias_out
    unit_one, scale_one = norm_parts(x_ref[...] + branch)
    normed = unit_one * gain_one + shift_one
    normed_b = normed.astype(BF)
    normed_ref[...] = normed_b
    downward = jnp.zeros(normed.shape, F32)
    for start in range(0, FF, FF_TILE):
        cols = slice(start, start + FF_TILE)
        upward = dot_nt(normed_b, wup_ref[cols, :]) + bup_ref[0:1, cols]
        hidden, slope = gelu_parts(upward)
        slope_ref[:, cols] = slope
        hidden_b = hidden.astype(BF)
        hidden_ref[:, cols] = hidden_b
        downward += dot_nn(hidden_b, wdown_ref[cols, :])
    unit_two, scale_two = norm_parts(normed + downward + bias_down)
    out_ref[...] = (unit_two * gain_two + shift_two).astype(BF)
    g_out = go_ref[...].astype(F32) * mask_ref[...].astype(F32)
    note(5, g_out * unit_two)
    note(6, g_out)
    g_mid = norm_back(g_out * gain_two, unit_two, scale_two)
    note(4, g_mid)
    g_mid_b = g_mid.astype(BF)
    gmid_ref[...] = g_mid_b
    g_normed = g_mid
    for start in range(0, FF, FF_TILE):
        cols = slice(start, start + FF_TILE)
        g_up = dot_nt(g_mid_b, wdown_ref[cols, :]) * slope_ref[:, cols]
        sums_ref[0:1, cols] += jnp.sum(g_up, 0, keepdims=True)
        g_up_b = g_up.astype(BF)
        gup_ref[:, cols] = g_up_b
        g_normed += dot_nn(g_up_b, wup_ref[cols, :])
    note(2, g_normed * unit_one)
    note(3, g_normed)
    g_first = norm_back(g_normed * gain_one, unit_one, scale_one)
    note(1, g_first)
    gfirst_ref[...] = g_first
    g_first_b = g_first.astype(BF)
    gfirstb_ref[...] = g_first_b
    gatt_ref[...] = dot_nn(g_first_b, wout_ref[...]).astype(BF)


def middle(attended, inputs, out_grad, masked, w_out, w_up, w_down, vecs, bias_up):
    rows = attended.shape[0]
    tile = ROW_TILE

    def row(width):
        return pl.BlockSpec((tile, width), lambda i: (i, 0))

    def whole(shape):
        return pl.BlockSpec(
            shape, lambda i: (0, 0), pipeline_mode=pl.Buffered(buffer_count=1)
        )

    return pl.pallas_call(
        middle_kernel,
        grid=(rows // tile,),
        in_specs=[
            row(D),
            row(D),
            row(D),
            row(1),
            whole((D, D)),
            whole((FF, D)),
            whole((FF, D)),
            whole((8, D)),
            whole((1, FF)),
        ],
        out_specs=[
            row(D),
            row(D),
            row(FF),
            row(D),
            row(FF),
            row(D),
            row(D),
            row(D),
            pl.BlockSpec((8, FF), lambda i: (0, 0)),
        ],
        out_shape=[
            jax.ShapeDtypeStruct((rows, D), BF),
            jax.ShapeDtypeStruct((rows, D), BF),
            jax.ShapeDtypeStruct((rows, FF), BF),
            jax.ShapeDtypeStruct((rows, D), BF),
            jax.ShapeDtypeStruct((rows, FF), BF),
            jax.ShapeDtypeStruct((rows, D), F32),
            jax.ShapeDtypeStruct((rows, D), BF),
            jax.ShapeDtypeStruct((rows, D), BF),
            jax.ShapeDtypeStruct((8, FF), F32),
        ],
        scratch_shapes=[pltpu.VMEM((tile, FF), F32)],
        compiler_params=pltpu.CompilerParams(vmem_limit_bytes=56 * MB),
        name="middle",
    )(attended, inputs, out_grad, masked, w_out, w_up, w_down, vecs, bias_up)


def gather_ids(chosen, places):
    return jnp.concatenate([chosen, places])


def slots_of(ids, owned):
    count = ids.shape[0]
    order = jnp.arange(count, dtype=jnp.int32)
    repeated = jnp.any(
        (ids[:, None] == ids[None, :]) & (order[:, None] < order[None, :]), axis=0
    )
    first = jnp.logical_not(repeated)
    base = (ids // owned) * owned
    below = (
        first[:, None]
        & (ids[:, None] >= base[None, :])
        & (ids[:, None] < ids[None, :])
    )
    return jnp.sum(below.astype(jnp.int32), axis=0)


def requests_of(ids, owner, slot, owned, devices, start, room):
    key = jnp.where((slot >= start) & (slot < start + room), owner * room + slot - start, -1)
    spots = jnp.arange(devices * room, dtype=jnp.int32)
    asked = jnp.max(
        jnp.where(key[:, None] == spots[None, :], (ids - owner * owned)[:, None], -1), axis=0
    )
    return key, asked


def pick(index, amount):
    return (index[:, None] == jnp.arange(amount, dtype=jnp.int32)[None, :]).astype(BF)


def adam_direction(param, first, second, grad, corr_one, corr_two, decay):
    first_next = beta_one * first + (1.0 - beta_one) * grad
    second_next = beta_two * second + (1.0 - beta_two) * grad * grad
    update = first_next / corr_one / (jnp.sqrt(second_next / corr_two) + adam_eps)
    return (update + decay * param, first_next)


def body(
    devices,
    token_ids,
    masked,
    swap_kind,
    swap_ids,
    out_grad,
    embed_table,
    table_first,
    table_second,
    layer_mats,
    mats_first,
    mats_second,
    layer_vecs,
    vecs_first,
    vecs_second,
):
    axis = "fsdp"
    rows = token_ids.shape[0]
    seqs = rows // LENGTH
    owned = embed_table.shape[0]
    share = LENGTH // devices
    me = lax.axis_index(axis)
    replaced = jnp.where(swap_kind < 8, mask_token, jnp.where(swap_kind == 8, swap_ids, token_ids))
    chosen = jnp.where(masked == 1, replaced, token_ids)

    room = 16 * -(-1536 // (16 * devices))
    more = 16
    my_places = VOCAB + me * share + jnp.arange(share, dtype=jnp.int32)
    ids = gather_ids(chosen, my_places)
    owner = ids // owned
    slot = slots_of(ids, owned)
    most = jnp.max(slot) + 1
    key, asked = requests_of(ids, owner, slot, owned, devices, 0, room)
    table_b = embed_table.astype(BF)

    def swap(blocks):
        return lax.all_to_all(blocks, axis, 0, 0, tiled=True)

    notes = jnp.concatenate(
        [asked.reshape(devices, room), jnp.full((devices, 1), most, jnp.int32)], axis=1
    )
    notes = swap(notes)
    wanted = notes[:, :room].reshape(-1)
    longest = jnp.max(notes[:, room])
    found = dot_nn(pick(wanted, owned), table_b).astype(BF)
    found = swap(found.reshape(devices, room, D)).reshape(-1, D)
    got = dot_nn(pick(key, devices * room), found)
    rounds = (longest - room + more - 1) // more

    def fetch_more(state):
        turn, got = state
        key, asked = requests_of(ids, owner, slot, owned, devices, room + turn * more, more)
        wanted = swap(asked.reshape(devices, more)).reshape(-1)
        found = dot_nn(pick(wanted, owned), table_b).astype(BF)
        found = swap(found.reshape(devices, more, D)).reshape(-1, D)
        return turn + 1, got + dot_nn(pick(key, devices * more), found)

    _, got = lax.while_loop(lambda state: state[0] < rounds, fetch_more, (jnp.int32(0), got))
    place_rows = lax.all_gather(got[rows:].astype(BF), axis, axis=0, tiled=True)
    inputs = (
        got[:rows].reshape(seqs, LENGTH, D) + place_rows.astype(F32)[None]
    ).reshape(rows, D)
    inputs_b = inputs.astype(BF)

    mats_t = lax.all_gather(layer_mats.astype(BF).T, axis, axis=0, tiled=True)
    vecs = lax.all_gather(layer_vecs.astype(BF), axis, axis=0, tiled=True).astype(F32)
    w_qkv = mats_t[:QKV]
    w_out = mats_t[QKV : QKV + D]
    w_up = mats_t[QKV + D : QKV + D + FF]
    w_down = mats_t[QKV + D + FF :]
    bias_qkv = jnp.concatenate([vecs[:D], jnp.zeros((D,), F32), vecs[D : 2 * D]])
    bias_up = vecs[5 * D : 5 * D + FF][None]
    small = jnp.concatenate(
        [vecs[2 * D : 5 * D], vecs[5 * D + FF :], jnp.zeros((2 * D,), F32)]
    ).reshape(8, D)

    projected = (dot_nt(inputs_b, w_qkv) + bias_qkv).astype(BF)
    attended, lse = attention_forward(projected)
    (
        outputs,
        normed_b,
        hidden_b,
        g_mid_b,
        g_up_b,
        g_first,
        g_first_b,
        g_att_b,
        sums,
    ) = middle(
        attended, inputs, out_grad, masked[:, None], w_out, w_up, w_down, small, bias_up
    )
    g_w_up = dot_tn(g_up_b, normed_b).astype(BF)
    g_w_down = dot_tn(hidden_b, g_mid_b).astype(BF)
    g_w_out = dot_tn(g_first_b, attended).astype(BF)
    g_proj, bias_sums = attention_backward(projected, attended, g_att_b, lse)
    g_in = g_first
    g_w_qkv = []
    for part in range(3):
        g_in = g_in + dot_nn(g_proj[part], w_qkv[part * D : (part + 1) * D])
        g_w_qkv.append(dot_tn(g_proj[part], inputs_b).astype(BF))
    input_grad = g_in.astype(BF)

    g_mats = jnp.concatenate(g_w_qkv + [g_w_out, g_w_up, g_w_down], axis=0)
    mats_grad = (
        lax.psum_scatter(g_mats, axis, scatter_dimension=0, tiled=True).astype(F32).T
    )
    g_vecs = jnp.concatenate(
        [
            bias_sums[0],
            bias_sums[1],
            sums[1, :D],
            sums[2, :D],
            sums[3, :D],
            sums[0],
            sums[4, :D],
            sums[5, :D],
            sums[6, :D],
        ]
    )
    vecs_grad = lax.psum_scatter(g_vecs, axis, scatter_dimension=0, tiled=True)

    g_place = jnp.sum(g_in.reshape(seqs, LENGTH, D), 0).astype(BF)
    g_place = lax.psum_scatter(g_place, axis, scatter_dimension=0, tiled=True)
    g_ids = jnp.concatenate([input_grad, g_place], axis=0)
    sent = dot_tn(pick(key, devices * room), g_ids).astype(BF)
    sent = swap(sent.reshape(devices, room, D)).reshape(-1, D)
    table_grad = dot_tn(pick(wanted, owned), sent)

    def send_more(state):
        turn, total = state
        key, asked = requests_of(ids, owner, slot, owned, devices, room + turn * more, more)
        wanted = swap(asked.reshape(devices, more)).reshape(-1)
        sent = dot_tn(pick(key, devices * more), g_ids).astype(BF)
        sent = swap(sent.reshape(devices, more, D)).reshape(-1, D)
        return turn + 1, total + dot_tn(pick(wanted, owned), sent)

    _, table_grad = lax.while_loop(
        lambda state: state[0] < rounds, send_more, (jnp.int32(0), table_grad)
    )

    counter = jnp.float32(STEP)
    corr_one = 1.0 - jnp.power(jnp.float32(beta_one), counter)
    corr_two = 1.0 - jnp.power(jnp.float32(beta_two), counter)
    table_step, table_first_next = adam_direction(
        embed_table, table_first, table_second, table_grad, corr_one, corr_two, decay_rate
    )
    mats_step, mats_first_next = adam_direction(
        layer_mats, mats_first, mats_second, mats_grad, corr_one, corr_two, decay_rate
    )
    vecs_step, vecs_first_next = adam_direction(
        layer_vecs, vecs_first, vecs_second, vecs_grad, corr_one, corr_two, 0.0
    )
    return (
        outputs,
        input_grad,
        table_grad,
        mats_grad,
        vecs_grad,
        table_step,
        table_first_next,
        mats_step,
        mats_first_next,
        vecs_step,
        vecs_first_next,
    )


def solution(mesh):
    line = P("fsdp")
    by_rows = P("fsdp", None)
    by_cols = P(None, "fsdp")
    return jax.shard_map(
        functools.partial(body, mesh.shape["fsdp"]),
        mesh=mesh,
        in_specs=(
            line,
            line,
            line,
            line,
            by_rows,
            by_rows,
            by_rows,
            by_rows,
            by_cols,
            by_cols,
            by_cols,
            line,
            line,
            line,
        ),
        out_specs=(
            by_rows,
            by_rows,
            by_rows,
            by_cols,
            line,
            by_rows,
            by_rows,
            by_cols,
            by_cols,
            line,
            line,
        ),
        check_vma=False,
    )
```

time: 1900 us -> 724 us (0.38)
  local copies, waits for them, and re-layouts: 595 us -> 19.1 us
  waiting for transfers between devices: 644 us -> 117 us
  matrix products: 343 us -> 107 us
  blocking collectives: 82.1 us -> 252 us
  other arithmetic: 195 us -> 34.7 us
  Pallas kernels: 0 us -> 156 us
    dynamic_update_slice x8 -> x0, local copies, waits for them, and re-layouts: 402 us -> none  [body(): lax.map(attention_backward, (query, keys, values, logsum, grad_att_b))]
    reduce_scatter x1 -> x2, waiting for transfers between devices: 399 us -> 110 us  [the longest x1 62.9 us: body(): lax.psum_scatter(g_mats, axis, scatter_dimension=0, tiled=True).astype(F32)]
    dot_general x40 -> x14, matrix products: 343 us -> 107 us  [the longest x8 62.1 us: dot_tn(): lax.dot_general(left, right, (((0,), (0,)), ((), ())), preferred_element_...]
    all_gather x2 -> x1, waiting for transfers between devices: 160 us -> 0.01 us  [body(): mats_t = lax.all_gather(layer_mats.astype(BF).T, axis, axis=0, tiled=True)]
    pallas_call x0 -> x3, Pallas kernels: none -> 156 us  [the longest x1 78.2 us: middle(): pl.pallas_call(middle_kernel, grid=(rows // tile,), in_specs=[row(D), row...]
    unnamed x2, blocking collectives: 82.1 us -> 209 us
    unnamed x5 -> x3, waiting for transfers between devices: 84.9 us -> 0.05 us
    scatter-add x2 -> x0, other arithmetic: 82.7 us -> none  [body(): jnp.zeros((TABLE, D), jnp.float32).at[chosen].add(grad_inputs).at[places]]
  transfers between devices with their start and end apart: 4 -> 6, of which waited for: 4 -> 3; matrix products, arithmetic and copies ran while one was open for 11% -> 14% of each run, Pallas kernels for 0% -> 0%
where the time goes in v1:
time: 724 us; the launch traced here: 716 us
  blocking collectives  252 us (35%)
  Pallas kernels  156 us (22%)
  waiting for transfers between devices  117 us (16%)
  matrix products  107 us (15%)
  other arithmetic  34.7 us (5%)
  local copies, waits for them, and re-layouts  19.1 us (3%)
  between operations  15.8 us (2%)
  starting transfers between devices  14.3 us (2%)
    unnamed x2, blocking collectives  209 us
    pallas_call x1, Pallas kernels, middle(): pl.pallas_call(middle_kernel, grid=(rows // tile,), in_specs=[row(D), row...  78.2 us
    reduce_scatter x1, waiting for transfers between devices, body(): lax.psum_scatter(g_mats, axis, scatter_dimension=0, tiled=True).astype(F32)  62.9 us
    dot_general x8, matrix products, dot_tn(): lax.dot_general(left, right, (((0,), (0,)), ((), ())), preferred_element_...  62.1 us
    reduce_scatter x1, waiting for transfers between devices, body(): g_place = lax.psum_scatter(g_place, axis, scatter_dimension=0, tiled=True)  47.2 us
    pallas_call x1, Pallas kernels, attention_backward(): pl.pallas_call(attention_backward_kernel, grid=(pairs, seqs), in_specs=[p...  44 us
    all_gather x1, blocking collectives, body(): place_rows = lax.all_gather(got[rows:].astype(BF), axis, axis=0, tiled=True)  43 us
    pallas_call x1, Pallas kernels, attention_forward(): pl.pallas_call(attention_forward_kernel, grid=(seqs, pairs), in_specs=[pl...  33.6 us
  transfers between devices with their start and end apart: 6, of which 3 were waited for; matrix products, arithmetic and copies ran while one was open for 14% of the time, Pallas kernels for 0%

profile of v1, /device:TPU:0, one launch (start us, length us, event | category | flops | bytes accessed | tf_op | source)
XLA Modules:
  0.0 715.9 jit_solution(15660592998517377799)
XLA Ops:
  11.6 4.8 convert_reduce_fusion
  20.6 7.3 %all-to-all-start.4 = ((s32[32,1,49]{2,1,0:T(1,128)}), s32[32,1,49]{2,1,0:T(1,128)S(1)}, u32[]{:S(2)}, u32[]{:S(2)}) async-start(s32[32,1,49]{2,1,0:T(1,128)} %bitcast.6), calls=%async_computation.4 | async-start | bytes 32768 | tf_op jit(solution)/shard_map/all_to_all | solution.py:402
  28.0 7.0 all-to-all-done.4
  43.2 123.1 %all-reduce.1 = bf16[9216]{0:T(1024)(128)(2,1)S(1)} all-reduce(bf16[9216]{0:T(1024)(128)(2,1)S(1)} %dynamic-update-slice), channel_id=1, replica_groups=mesh['fsdp'=32] {'fsdp'}, use_global_device_ids=true, to_apply=%add.1 | all-reduce | flops 9216 | bytes 36864
  169.0 7.6 %fusion.9 = f32[2064,768]{1,0:T(8,128)} fusion(bf16[1536,768]{1,0:T(8,128)(2,1)S(1)} %bitcast.96, s32[2064]{0:T(1024)S(1)} %get-tuple-element.280), kind=kOutput, calls=%fused_computation.27 | convolution fusion | flops 4872757248 | bytes 8708160 | tf_op jit(solution)/shard_map/dot_general | solution.py:37
  177.8 43.0 %all_gather.9 = bf16[512,768]{1,0:T(8,128)(2,1)S(1)} all-gather(bf16[16,768]{1,0:T(8,128)(2,1)S(1)} %slice.189), channel_id=1, replica_groups=mesh['fsdp'=32] {'fsdp'}, dimensions={0}, use_global_device_ids=true | all-gather | bytes 811008 | tf_op jit(solution)/shard_map/all_gather | solution.py:424
  220.9 6.4 fusion.80
  227.3 13.1 %add_convert_fusion.q_ref.k_ref.v_ref = bf16[2048,2304]{1,0:T(8,128)(2,1)} fusion(bf16[2048,768]{1,0:T(8,128)(2,1)S(1)} %get-tuple-element.267, f32[2304]{0:T(1024)S(1)} %pad_maximum_fusion.2, bf16[9216,768]{1,0:T(8,128)(2,1)} %all-gather.2.cloned.1.call-done), kind=kOutput, calls=%fused_computation.19 | convolution fusion | flops 7257194496 | bytes 16131072 | tf_op jit(solution)/shard_map/dot_general | solution.py:43
  240.3 33.6 %attention_forward.1 = (bf16[2048,768]{1,0:T(8,128)(2,1)S(1)}, f32[24,2,512]{2,1,0:T(2,128)S(1)}) custom-call(bf16[2048,2304]{1,0:T(8,128)(2,1)} %add_convert_fusion.q_ref.k_ref.v_ref, bf16[2048,2304]{1,0:T(8,128)(2,1)} %add_convert_fusion.q_ref.k_ref.v_ref, bf16[2048,2304]{1,0:T(8,128)(2,1)} %add_convert_fusion.q_ref.k_ref.v_ref), custom_call_target="tpu_custom_call" | custom-call | tf_op jit(solution)/shard_map/attention_forward/pallas_call | solution.py:78
  278.0 8.0 %fusion.81 = (bf16[3072,768]{1,0:T(8,128)(2,1)}, bf16[3072,768]{1,0:T(8,128)(2,1)}) fusion(bf16[9216,768]{1,0:T(8,128)(2,1)} %all-gather.2.cloned.1.call-done), kind=kLoop, calls=%fused_computation.133 | loop fusion | bytes 18874368 | tf_op jit(solution)/shard_map/slice | solution.py:435
  286.0 78.2 %middle.1 = (bf16[2048,768]{1,0:T(8,128)(2,1)}, bf16[2048,768]{1,0:T(8,128)(2,1)}, bf16[2048,3072]{1,0:T(8,128)(2,1)}, bf16[2048,768]{1,0:T(8,128)(2,1)}, bf16[2...) custom-call(bf16[2048,768]{1,0:T(8,128)(2,1)} %copy-done, ...), custom_call_target="tpu_custom_call" | custom-call | tf_op jit(solution)/shard_map/middle/pallas_call | solution.py:283
  364.1 44.0 %attention_backward.1 = (bf16[3,2048,768]{2,1,0:T(8,128)(2,1)}, f32[8,768]{1,0:T(8,128)S(1)}) custom-call(bf16[2048,2304]{1,0:T(8,128)(2,1)} %add_convert_fusion.q_ref.k_ref.v_ref, bf16[2048,2304]{1,0:T(8,128)(2,1)} %add_convert_fusion.q_ref.k_ref.v_ref, bf16[2048,2304]{1,0:T(8,128)(2,1)} %add_convert_fusion.q_ref.k_ref.v_ref, ...), custom_call_target="tpu_custom_call" | custom-call | tf_op jit(solution)/shard_map/attention_backward/pallas_call | solution.py:143
  408.1 5.7 fusion.39
  418.0 5.9 fusion.25
  423.9 11.3 %fusion.85 = (bf16[2048,768]{1,0:T(8,128)(2,1)}, f32[2048,768]{1,0:T(8,128)}) fusion(bf16[9216,768]{1,0:T(8,128)(2,1)} %all-gather.2.cloned.1.call-done, bf16[3,2048,768]{2,1,0:T(8,128)(2,1)} %get-tuple-element.214, f32[2048,768]{1,0:T(8,128)S(1)} %fusion.21, f32[2048,768]{1,0:T(8,128)S(1)} %bitcast.95, f32[2048,768]{1,0:T(8,128)} %fusion.25), kind=kOutput, calls=%fused_computation.137 | convolution fusion | flops 2422210560 | bytes 32636928 | tf_op jit(solution)/shard_map/dot_general | solution.py:37
  439.9 6.8 fusion.45
  446.7 5.8 fusion.51
  456.3 15.3 %fusion.13 = bf16[9216,768]{1,0:T(8,128)(2,1)} fusion(bf16[9216,768]{1,0:T(8,128)(2,1)} %fusion.54, bf16[2048,3072]{1,0:T(8,128)(2,1)S(1)} %bitcast.108, bf16[2048,768]{1,0:T(8,128)(2,1)} %get-tuple-element.218), kind=kOutput, calls=%fused_computation.35 | convolution fusion | flops 9666035712 | bytes 20447232 | tf_op jit(solution)/shard_map/dot_general | solution.py:49
  471.6 12.5 %fusion.12 = bf16[9216,768]{1,0:T(8,128)(2,1)} fusion(bf16[9216,768]{1,0:T(8,128)(2,1)} %fusion.13, bf16[2048,3072]{1,0:T(8,128)(2,1)S(1)} %bitcast.106, bf16[2048,768]{1,0:T(8,128)(2,1)S(1)} %copy-done.21), kind=kOutput, calls=%fused_computation.33 | convolution fusion | flops 9666035712 | bytes 20447232 | tf_op jit(solution)/shard_map/dot_general | solution.py:49
  484.2 47.2 %reduce-scatter.3.cloned.1.call-done = bf16[16,768]{1,0:T(8,128)(2,1)} async-done(((bf16[512,768]{1,0:T(8,128)(2,1)}), bf16[16,768]{1,0:T(8,128)(2,1)}) %reduce-scatter.3.cloned.1.call-update) | async-done | bytes 24592 | tf_op jit(solution)/shard_map/reduce_scatter | solution.py:488
  531.4 8.8 %fusion.15 = bf16[1536,768]{1,0:T(8,128)(2,1)} fusion(s32[2064]{0:T(1024)S(1)} %copy-done.14, bf16[16,768]{1,0:T(8,128)(2,1)} %reduce-scatter.3.cloned.1.call-done, bf16[2048,768]{1,0:T(8,128)(2,1)S(1)} %copy-done.3), kind=kOutput, calls=%fused_computation.37 | convolution fusion | flops 4880277504 | bytes 5537856 | tf_op jit(solution)/shard_map/dot_general | solution.py:49
  546.0 85.5 %all-reduce.2 = f32[9216]{0:T(1024)S(1)} all-reduce(f32[9216]{0:T(1024)S(1)} %constant_dynamic-update-slice_fusion.5), channel_id=4, replica_groups=mesh['fsdp'=32] {'fsdp'}, use_global_device_ids=true, to_apply=%region_14.15.clone | all-reduce | flops 9216 | bytes 73728
  637.7 5.6 fusion.61
  643.3 62.9 %reduce-scatter.5.cloned.1.call-done = bf16[288,768]{1,0:T(8,128)(2,1)} async-done(((bf16[9216,768]{1,0:T(8,128)(2,1)}), bf16[288,768]{1,0:T(8,128)(2,1)}) %reduce-scatter.5.cloned.1.call-update) | async-done | bytes 442384 | tf_op jit(solution)/shard_map/reduce_scatter | solution.py:470
  (127 shorter events, 50.9 us)
Async XLA Ops:
  7.2 20.7 %copy-start.4 = (f32[472,768]{1,0:T(8,128)S(1)}, f32[472,768]{1,0:T(8,128)}, u32[]{:S(2)}) copy-start(f32[472,768]{1,0:T(8,128)} %param.23) | copy-start | bytes 4349956
  7.2 220.1 %all-gather.2.cloned.1.call-start = ((), (), s32[]{:S(2)}) async-start(), calls=%async_computation.9 | async-start | bytes 14598144 | tf_op jit(solution)/shard_map/all_gather | solution.py:430
  17.0 151.9 %copy-start.13 = (s32[2064]{0:T(1024)}, s32[2064]{0:T(1024)S(1)}, u32[]{:S(2)}) copy-start(s32[2064]{0:T(1024)S(1)} %get-tuple-element.280) | copy-start | bytes 24772
  20.6 14.4 %all-to-all-start.4 = ((s32[32,1,49]{2,1,0:T(1,128)}), s32[32,1,49]{2,1,0:T(1,128)S(1)}, u32[]{:S(2)}, u32[]{:S(2)}) async-start(s32[32,1,49]{2,1,0:T(1,128)} %bitcast.6), calls=%async_computation.4 | async-start | bytes 32768 | tf_op jit(solution)/shard_map/all_to_all | solution.py:402
  38.6 130.3 %all-to-all-start.5 = ((bf16[32,48,768]{2,1,0:T(8,128)(2,1)}), bf16[32,48,768]{2,1,0:T(8,128)(2,1)S(1)}, u32[]{:S(2)}, u32[]{:S(2)}) async-start(bf16[32,48,768]{2,1,0:T(8,128)(2,1)} %bitcast.97), calls=%async_computation.5 | async-start | bytes 4718592 | tf_op jit(solution)/shard_map/all_to_all | solution.py:402
  41.5 489.8 %reduce-scatter.3.cloned.1.call-start = ((), (), s32[]{:S(2)}) async-start(), calls=%async_computation.10 | async-start | bytes 811008 | tf_op jit(solution)/shard_map/reduce_scatter | solution.py:488
  286.0 78.2 %copy-start.1 = (bf16[2048,768]{1,0:T(8,128)(2,1)S(1)}, bf16[2048,768]{1,0:T(8,128)(2,1)}, u32[]{:S(2)}) copy-start(bf16[2048,768]{1,0:T(8,128)(2,1)} %copy-done) | copy-start | bytes 9437188
  364.1 44.0 %copy-start.7 = (bf16[2048,768]{1,0:T(8,128)(2,1)S(1)}, bf16[2048,768]{1,0:T(8,128)(2,1)}, u32[]{:S(2)}) copy-start(bf16[2048,768]{1,0:T(8,128)(2,1)} %copy-done.6) | copy-start | bytes 9437188
  439.6 266.6 %reduce-scatter.5.cloned.1.call-start = ((), (), s32[]{:S(2)}) async-start(), calls=%async_computation.11 | async-start | bytes 14598144 | tf_op jit(solution)/shard_map/reduce_scatter | solution.py:470
  439.9 16.4 %slice-start.5 = ((s8[12582912]{0:T(1024)(128)(4,1)}), s8[4194304]{0:T(1024)(128)(4,1)S(1)}, s32[]{:S(2)}) async-start(s8[12582912]{0:T(1024)(128)(4,1)} %bitcast.107), calls=%async_computation.17 | async-start | bytes 8388608
  439.9 16.4 %slice-start.6 = ((s8[12582912]{0:T(1024)(128)(4,1)}), s8[4194304]{0:T(1024)(128)(4,1)S(1)}, s32[]{:S(2)}) async-start(s8[12582912]{0:T(1024)(128)(4,1)} %bitcast.107), calls=%async_computation.18 | async-start | bytes 8388608
  452.5 19.2 %slice-start.2 = ((s8[12582912]{0:T(1024)(128)(4,1)}), s8[4194304]{0:T(1024)(128)(4,1)S(1)}, s32[]{:S(2)}) async-start(s8[12582912]{0:T(1024)(128)(4,1)} %bitcast.105), calls=%async_computation.14 | async-start | bytes 8388608
  456.3 15.3 %slice-start.3 = ((s8[12582912]{0:T(1024)(128)(4,1)}), s8[4194304]{0:T(1024)(128)(4,1)S(1)}, s32[]{:S(2)}) async-start(s8[12582912]{0:T(1024)(128)(4,1)} %bitcast.105), calls=%async_computation.15 | async-start | bytes 8388608
  456.3 15.3 %slice-start.4 = ((s8[12582912]{0:T(1024)(128)(4,1)}), s8[4194304]{0:T(1024)(128)(4,1)S(1)}, s32[]{:S(2)}) async-start(s8[12582912]{0:T(1024)(128)(4,1)} %bitcast.105), calls=%async_computation.16 | async-start | bytes 8388608
  456.3 15.3 %copy-start.21 = (bf16[2048,768]{1,0:T(8,128)(2,1)S(1)}, bf16[2048,768]{1,0:T(8,128)(2,1)}, u32[]{:S(2)}) copy-start(bf16[2048,768]{1,0:T(8,128)(2,1)} %get-tuple-element.220) | copy-start | bytes 9437188
  484.1 47.3 %copy-start.3 = (bf16[2048,768]{1,0:T(8,128)(2,1)S(1)}, bf16[2048,768]{1,0:T(8,128)(2,1)}, u32[]{:S(2)}) copy-start(bf16[2048,768]{1,0:T(8,128)(2,1)} %get-tuple-element.285) | copy-start | bytes 9437188
  484.1 47.3 %copy-start.14 = (s32[2064]{0:T(1024)S(1)}, s32[2064]{0:T(1024)}, u32[]{:S(2)}) copy-start(s32[2064]{0:T(1024)} %copy-done.13) | copy-start | bytes 24772
  540.2 91.3 %copy-start.18 = (f32[288]{0:T(512)S(1)}, f32[288]{0:T(512)}, u32[]{:S(2)}) copy-start(f32[288]{0:T(512)} %param.29) | copy-start | bytes 3460
  540.2 91.4 %copy-start.19 = (f32[288]{0:T(512)S(1)}, f32[288]{0:T(512)}, u32[]{:S(2)}) copy-start(f32[288]{0:T(512)} %param.31) | copy-start | bytes 3460
  540.2 91.4 %copy-start.20 = (f32[288]{0:T(512)S(1)}, f32[288]{0:T(512)}, u32[]{:S(2)}) copy-start(f32[288]{0:T(512)} %param.30) | copy-start | bytes 3460
  540.2 92.1 %copy-start.12 = (bf16[16,768]{1,0:T(8,128)(2,1)S(1)}, bf16[16,768]{1,0:T(8,128)(2,1)}, u32[]{:S(2)}) copy-start(bf16[16,768]{1,0:T(8,128)(2,1)} %reduce-scatter.3.cloned.1.call-done) | copy-start | bytes 73732
  540.2 93.9 %all-to-all-start.6 = ((bf16[32,48,768]{2,1,0:T(8,128)(2,1)}), bf16[32,48,768]{2,1,0:T(8,128)(2,1)}, u32[]{:S(2)}, u32[]{:S(2)}) async-start(bf16[32,48,768]{2,1,0:T(8,128)(2,1)} %bitcast.98), calls=%async_computation.7 | async-start | bytes 4718592 | tf_op jit(solution)/shard_map/all_to_all | solution.py:402
  637.6 68.5 %copy-start.5 = (f32[768,288]{0,1:T(8,128)S(1)}, f32[768,288]{0,1:T(8,128)}, u32[]{:S(2)}) copy-start(f32[768,288]{0,1:T(8,128)} %param.26) | copy-start | bytes 2654212
  637.6 68.5 %copy-start.10 = (f32[768,288]{0,1:T(8,128)S(1)}, f32[768,288]{0,1:T(8,128)}, u32[]{:S(2)}) copy-start(f32[768,288]{0,1:T(8,128)} %param.28) | copy-start | bytes 2654212
  (13 other events, 72.6 us)
Sparse Core Ops, SparseCore 0:
  11.5 145.0 all-gather.1
  439.7 91.6 reduce-scatter.2
  537.4 168.7 reduce-scatter.4
